TPU v7x, 32 devices: a whole 2x2x4 slice. The times are simulated.
32 devices in a mesh: event: 4 (over x, core), space: 8 (over z, y).
Axes of the slice: x: 2, y: 2, z: 4, core: 2. Of those that a mesh axis runs over, the one named last changes fastest.
Arguments:
- state_now: float32 [4, 64, 16, 512], P('event', 'space'), may hold values from -6 to 6
- state_prev: float32 [4, 64, 16, 512], P('event', 'space'), may hold values from -6 to 6
- adjoint_now: float32 [4, 64, 16, 512], P('event', 'space'), may hold values from -1.8 to 1.8
- adjoint_next: float32 [4, 64, 16, 512], P('event', 'space'), may hold values from -1.8 to 1.8
- modulus: float32 [5, 16, 5, 4, 5, 128], P(None, 'space'), may hold values from 0.5 to 2
- density: float32 [64, 16, 512], P('space'), may hold values from 0.5 to 2
- receivers: int32 [1024], P('space'), may hold values from 0 to 65535
- observed: float32 [4, 3, 1024], P('event', None, 'space'), may hold values from -12 to 12
Outputs:
- kernel: float32 [5, 16, 5, 4, 5, 128], P(None, 'space', None, 'event')
- misfit: float32 [4], P('event')
Inputs may be any that keep to these rules, and one draw needn't show every extreme that they name: A node of the receiver's own slab, numbered with the third index fastest over 8 x 16 x 512 nodes; two receivers may share a node.
All inputs are finite; a program needn't handle non-finite values. Where the computation divides by a largest or mean magnitude, that divisor is 1e-20 or more.
Results may differ from a plain program's by a relative error of at most 0.00011.
Values sent between devices are 32-bit elements; how exact they have to be, the bound alone decides.
A program may use at most 64 MiB of HBM per device.

v0:
```python
import math

import jax
import jax.numpy as jnp
import ml_dtypes
import numpy as np
from jax import lax
from jax.experimental import pallas as pl
from jax.experimental.pallas import tpu as pltpu
from jax.sharding import PartitionSpec as P

TIME_STEP = 0.05
EPSILON = 1e-06
LIMIT = 64 * 1024 * 1024 - 128 * 1024
F32 = jnp.float32
BF16 = jnp.bfloat16


def gll_tables():
    root = math.sqrt(3.0 / 7.0)
    points = np.array([-1.0, -root, 0.0, root, 1.0])
    weights = np.array([0.1, 49.0 / 90.0, 32.0 / 45.0, 49.0 / 90.0, 0.1])
    legendre = (35.0 * points**4 - 30.0 * points**2 + 3.0) / 8.0
    derivative = np.zeros((5, 5))
    for row in range(5):
        for column in range(5):
            if row != column:
                derivative[row, column] = legendre[row] / (
                    legendre[column] * (points[row] - points[column])
                )
    derivative[0, 0] = -5.0
    derivative[4, 4] = 5.0
    return derivative, weights


DERIVATIVE, WEIGHTS = gll_tables()
LINE = [0.2, 49.0 / 90.0, 32.0 / 45.0, 49.0 / 90.0]


def apply_line(matrix, v):
    m = matrix
    o0, o1 = v[0] - v[4], v[1] - v[3]
    e0, e1 = v[0] + v[4], v[1] + v[3]
    out = [None] * 5
    for s in (0, 1):
        odd = float((m[s, 0] - m[s, 4]) / 2) * o0 + float((m[s, 1] - m[s, 3]) / 2) * o1
        even = (
            float((m[s, 0] + m[s, 4]) / 2) * e0
            + float((m[s, 1] + m[s, 3]) / 2) * e1
            + float(m[s, 2]) * v[2]
        )
        out[s], out[4 - s] = odd + even, odd - even
    out[2] = float(m[2, 0]) * o0 + float(m[2, 1]) * o1
    return out


def thirds(x):
    high = x.astype(BF16)
    rest = x - high.astype(F32)
    mid = rest.astype(BF16)
    return high, mid, (rest - mid.astype(F32)).astype(BF16)


def dot(a, b):
    return jnp.dot(a, b, preferred_element_type=F32)


def dot_rows(a, b):
    return lax.dot_general(a, b, (((1,), (1,)), ((), ())), preferred_element_type=F32)


def tables(ex, ey, ez):
    ny, nz = 4 * ey, 4 * ez
    column = np.zeros((nz, nz), np.float32)
    for r in range(4):
        for l in range(ez):
            column[4 * l + r, r * ez + l] = 1
    rows = np.zeros((4 * ex * ny, 4 * ex * ny), np.float32)
    plane = np.zeros((32, ny), np.float32)
    for q in range(4):
        for j in range(ey):
            for i in range(ex):
                for p in range(4):
                    rows[(p * 4 + q) * 8 + i * ey + j, (i * 4 + p) * ny + j * 4 + q] = 1
            plane[q * 8 + (ex - 1) * ey + j, j * 4 + q] = 1
    cube = np.zeros((128, ez), np.float32)
    w = WEIGHTS
    cube[:125] = -(w[:, None, None] * w[None, :, None] * w[None, None, :]).reshape(125, 1)
    as_bf16 = [t.astype(ml_dtypes.bfloat16) for t in (column, rows, plane)]
    return as_bf16 + [cube]


def make_kernel(ex, ey, ez, steps, events, spaces, receivers_total):
    ny, nz = 4 * ey, 4 * ez
    half = (ex - 1) * ey
    shift_y = int(math.log2(nz))
    shift_x = shift_y + int(math.log2(ny))
    shift_j = int(math.log2(ey))
    last = steps - 1
    samples = steps * receivers_total

    def kernel(
        now_hbm, prev_hbm, adj_hbm, next_hbm, density_hbm, modulus_hbm, rec_hbm, obs_hbm,
        column_hbm, rows_hbm, plane_hbm, cube_hbm,
        out_ref, misfit_ref,
        fields, modulus_ref, rec_ref, obs_ref, column_ref, rows_ref, plane_ref, cube_ref, in_sem,
        halo, halo_rec, halo_obs, u, lam, before, scale, stiff, grads, force, total, inject,
        row_mask, lane_mask, row_mask_h, lane_mask_h,
        send_l, send_r, recv_l, recv_r, sums_out, sums_in, pack, got, relay, tops_out, tops_in, tops_far,
        final,
        halo_ss, halo_rs, ls, lr, rs, rr, sum_s, sum_r, red_s, red_r, top_s, top_r, far_s, far_r,
    ):
        me = lax.axis_index("space")
        event = lax.axis_index("event")
        left = jnp.maximum(me - 1, 0)
        right = jnp.minimum(me + 1, spaces - 1)
        has_left, has_right = me > 0, me < spaces - 1
        MESH = pl.DeviceIdType.MESH

        own = [r.at[0] for r in (now_hbm, adj_hbm, prev_hbm, next_hbm)] + [density_hbm]
        local = [(own[0], fields.at[0]), (rows_hbm, rows_ref), (column_hbm, column_ref)]
        local += [(plane_hbm, plane_ref), (own[1], fields.at[1]), (modulus_hbm, modulus_ref)]
        local += [(own[f], fields.at[f]) for f in (2, 3, 4)]
        local += [(rec_hbm, rec_ref), (obs_hbm, obs_ref), (cube_hbm, cube_ref)]
        local = [
            pltpu.make_async_copy(src, dst, in_sem.at[k]) for k, (src, dst) in enumerate(local)
        ]

        barrier = pltpu.get_barrier_semaphore()

        @pl.loop(1, spaces)
        def _(k):
            pl.semaphore_signal(
                barrier, inc=1, device_id={"space": lax.rem(me + k, spaces)}, device_id_type=MESH
            )

        for k in range(1, events):
            pl.semaphore_signal(
                barrier, inc=1, device_id={"event": lax.rem(event + k, events)}, device_id_type=MESH
            )

        for copy in local:
            copy.start()

        @pl.when(jnp.logical_not(has_right))
        def _():
            halo[0:4] = jnp.zeros((4, ny, nz), F32)
            halo[4] = jnp.ones((ny, nz), F32)
            halo_rec[...] = jnp.zeros_like(halo_rec)
            halo_obs[...] = jnp.zeros_like(halo_obs)
            recv_r[...] = jnp.zeros_like(recv_r)

        @pl.when(jnp.logical_not(has_left))
        def _():
            recv_l[...] = jnp.zeros_like(recv_l)

        pl.semaphore_wait(barrier, spaces - 1 + events - 1)

        def to_left(src, dst, ss, sr):
            return pltpu.make_async_remote_copy(
                src_ref=src, dst_ref=dst, send_sem=ss, recv_sem=sr,
                device_id={"space": left}, device_id_type=MESH,
            )

        def to_right(src, dst, ss, sr):
            return pltpu.make_async_remote_copy(
                src_ref=src, dst_ref=dst, send_sem=ss, recv_sem=sr,
                device_id={"space": right}, device_id_type=MESH,
            )

        halo_copies = [
            to_left(own[f].at[0], halo.at[f], halo_ss.at[f], halo_rs.at[f]) for f in range(5)
        ]
        halo_copies.append(to_left(rec_hbm, halo_rec, halo_ss.at[5], halo_rs.at[5]))
        halo_copies.append(to_left(obs_hbm, halo_obs, halo_ss.at[6], halo_rs.at[6]))

        @pl.when(has_left)
        def _():
            for copy in halo_copies:
                copy.start()

        def halo_wait(numbers):
            @pl.when(has_right)
            def _():
                for k in numbers:
                    halo_copies[k].wait_recv()

        def share(slot, k):
            there = lax.rem(me + k, spaces)
            return pltpu.make_async_remote_copy(
                src_ref=sums_out.at[slot], dst_ref=sums_in.at[slot, me],
                send_sem=sum_s.at[slot, k], recv_sem=sum_r.at[slot, me],
                device_id={"space": there}, device_id_type=MESH,
            )

        def taken(slot, k):
            there = lax.rem(me + k, spaces)
            return pltpu.make_async_remote_copy(
                src_ref=sums_out.at[slot], dst_ref=sums_in.at[slot, there],
                send_sem=sum_s.at[slot, k], recv_sem=sum_r.at[slot, there],
                device_id={"space": there}, device_id_type=MESH,
            )

        def share_all(slot, lanes):
            tile = jnp.broadcast_to(lanes, (8, lanes.shape[1]))
            sums_out[slot] = tile
            sums_in[slot, me] = tile

            @pl.loop(1, spaces)
            def _(k):
                share(slot, k).start()

        def take_all(slot):
            @pl.loop(1, spaces)
            def _(k):
                copy = taken(slot, k)
                copy.wait_send()
                copy.wait_recv()

            tile = jnp.sum(sums_in[slot], axis=0)
            return jnp.sum(tile[0:1, :], axis=1, keepdims=True)

        def iota(shape, axis):
            return lax.broadcasted_iota(jnp.int32, shape, axis)

        def target(f):
            if f < 2:
                return (u, lam)[f].at[0]
            return before.at[f - 2] if f < 4 else scale

        def order(nodes, rows):
            count = rows.shape[0]
            parts = [dot(rows[...], part).astype(BF16) for part in thirds(nodes)]
            x = dot(jnp.concatenate(parts, axis=0), column_ref[...])
            return x[:count] + x[count : 2 * count] + x[2 * count :]

        def order_own(f):
            values = order(fields[f].reshape(4 * ex * ny, nz), rows_ref)
            for r in range(4):
                part = values[:, r * ez : (r + 1) * ez]
                target(f)[0:4, 0:4, r] = part.reshape(4, 4, 8, ez)

        def order_halo(f):
            values = order(halo[f], plane_ref)
            for r in range(4):
                part = values[:, r * ez : (r + 1) * ez]
                target(f)[4, 0:4, r] = part.reshape(4, 8, ez)

        def set_stiffness():
            for p in range(5):
                for q in range(5):
                    for r in range(5):
                        w = float(WEIGHTS[p] * WEIGHTS[q] * WEIGHTS[r])
                        for i in range(ex):
                            stiff[p, q, r, i * ey : (i + 1) * ey, :] = modulus_ref[p, i, q, r] * w

        def masks(rec, rows_out, lanes_out, plane_only):
            x = lax.shift_right_logical(rec, shift_x)
            y = lax.shift_right_logical(rec, shift_y) & (ny - 1)
            z = rec & (nz - 1)
            p, i = x & 3, lax.shift_right_logical(x, 2)
            q, j = y & 3, lax.shift_right_logical(y, 2)
            r, l = z & 3, lax.shift_right_logical(z, 2)
            if plane_only:
                row = (q * 4 + r) * 8 + half + j
                row = jnp.where(x == 0, row, -1)
            else:
                row = ((p * 4 + q) * 4 + r) * 8 + i * ey + j
            shape = rows_out.shape
            rows_out[...] = jnp.where(iota(shape, 0) == jnp.broadcast_to(row, shape), 1.0, 0.0)
            shape = lanes_out.shape
            hit = jnp.where(iota(shape, 0) == jnp.broadcast_to(l, shape), 1.0, 0.0)
            lanes_out[...] = hit.astype(BF16)

        def set_scale():
            row8, lane8 = iota((8, ez), 0), iota((8, ez), 1)
            first_x = jnp.logical_and(row8 < ey, me == 0)
            half_x = jnp.where(first_x, 0.5, 1.0).astype(F32)
            half_y = jnp.where((row8 & (ey - 1)) == 0, 0.5, 1.0).astype(F32)
            half_z = jnp.where(lane8 == 0, 0.5, 1.0).astype(F32)
            kept = jnp.where(jnp.logical_and(row8 >= half, has_right), 1.0, 0.0).astype(F32)
            for p in range(5):
                for q in range(4):
                    for r in range(4):
                        weight = float(LINE[p % 4] * LINE[q] * LINE[r])
                        mass = scale[p, q, r] * weight if p < 4 else jnp.where(
                            row8 >= half, scale[p, q, r], 1.0) * weight
                        if p == 0:
                            mass = mass * half_x
                        if q == 0:
                            mass = mass * half_y
                        if r == 0:
                            mass = mass * half_z
                        value = (TIME_STEP * TIME_STEP) / mass
                        scale[p, q, r] = value * kept if p == 4 else value

        def turn(x, by, axis):
            shape = x.shape
            flat_x = x.reshape((-1,) + shape[-2:])
            pieces = [
                pltpu.roll(flat_x[n], by % shape[axis], axis + 2)[None] for n in range(flat_x.shape[0])
            ]
            return jnp.concatenate(pieces, axis=0).reshape(shape)

        def low(shape):
            return iota(shape, len(shape) - 2) < half

        def fill(e):
            shape = (4, 4, 8, ez)
            e[4, 0:4, 0:4] = jnp.where(
                low(shape), turn(e[0, 0:4, 0:4], -ey, -2), e[4, 0:4, 0:4]
            )
            shape = (5, 4, 8, ez)
            inner = (iota(shape, 2) & (ey - 1)) != ey - 1
            e[:, 4, 0:4] = jnp.where(inner, turn(e[:, 0, 0:4], -1, -2), 0.0)
            shape = (5, 5, 8, ez)
            e[:, :, 4] = jnp.where(iota(shape, 3) != ez - 1, turn(e[:, :, 0], -1, -1), 0.0)

        def stencil(e, f, store=None, partner=None, fresh=False):
            @pl.loop(0, 5)
            def _(q):
                g = apply_line(DERIVATIVE, [e[p, q] for p in range(5)])
                for p in range(5):
                    if store is not None:
                        store[0, p, q] = g[p]
                    if partner is not None:
                        product = g[p] * partner[0, p, q]
                        total[p, q] = product if fresh else total[p, q] + product
                if f is not None:
                    back = apply_line(DERIVATIVE.T, [stiff[p, q] * g[p] for p in range(5)])
                    for p in range(5):
                        f[p, q] = back[p]

            @pl.loop(0, 5)
            def _(p):
                g = apply_line(DERIVATIVE, [e[p, q] for q in range(5)])
                for q in range(5):
                    if store is not None:
                        store[1, p, q] = g[q]
                    if partner is not None:
                        total[p, q] = total[p, q] + g[q] * partner[1, p, q]
                if f is not None:
                    back = apply_line(DERIVATIVE.T, [stiff[p, q] * g[q] for q in range(5)])
                    for q in range(5):
                        f[p, q] = f[p, q] + back[q]
                g = apply_line(DERIVATIVE, [e[p, :, r] for r in range(5)])
                for r in range(5):
                    if store is not None:
                        store[2, p, :, r] = g[r]
                    if partner is not None:
                        total[p, :, r] = total[p, :, r] + g[r] * partner[2, p, :, r]
                if f is not None:
                    back = apply_line(DERIVATIVE.T, [stiff[p, :, r] * g[r] for r in range(5)])
                    for r in range(5):
                        f[p, :, r] = f[p, :, r] + back[r]

        def messages(m):
            return (
                to_left(send_l.at[m], recv_r.at[m], ls.at[m], lr.at[m]),
                to_right(send_r.at[m], recv_l.at[m], rs.at[m], rr.at[m]),
            )

        def assemble(f, m):
            shape = (5, 5, 8, ez)
            f[:, :, 0] = f[:, :, 0] + jnp.where(iota(shape, 3) != 0, turn(f[:, :, 4], 1, -1), 0.0)
            shape = (5, 4, 8, ez)
            inner = (iota(shape, 2) & (ey - 1)) != 0
            f[:, 0, 0:4] = f[:, 0, 0:4] + jnp.where(inner, turn(f[:, 4, 0:4], 1, -2), 0.0)
            pair = (2, 4, 8, ez)
            send_l[m] = jnp.where(low(pair), f[0, 0:2, 0:4], turn(f[0, 2:4, 0:4], half, -2))
            send_r[m] = jnp.where(low(pair), turn(f[4, 0:2, 0:4], half, -2), f[4, 2:4, 0:4])
            leftward, rightward = messages(m)

            @pl.when(has_left)
            def _():
                leftward.start()

            @pl.when(has_right)
            def _():
                rightward.start()

            shape = (4, 4, 8, ez)
            f[0, 0:4, 0:4] = f[0, 0:4, 0:4] + jnp.where(
                low(shape), 0.0, turn(f[4, 0:4, 0:4], ey, -2)
            )

        def receive(f, m):
            leftward, rightward = messages(m)

            @pl.when(has_left)
            def _():
                leftward.wait_send()
                rightward.wait_recv()

            @pl.when(has_right)
            def _():
                rightward.wait_send()
                leftward.wait_recv()

            pair = (2, 4, 8, ez)
            near = recv_l[m]
            f[0, 0:2, 0:4] = f[0, 0:2, 0:4] + jnp.where(low(pair), near, 0.0)
            f[0, 2:4, 0:4] = f[0, 2:4, 0:4] + jnp.where(low(pair), turn(near, half, -2), 0.0)
            far = recv_r[m]
            f[4, 0:2, 0:4] = f[4, 0:2, 0:4] + turn(far, half, -2)
            f[4, 2:4, 0:4] = f[4, 2:4, 0:4] + far

        def advance(new, current, old, f, count=5):
            for p in range(count):
                new[p, 0:4, 0:4] = (
                    2.0 * current[p, 0:4, 0:4]
                    - old[p, 0:4, 0:4]
                    - scale[p] * f[p, 0:4, 0:4]
                )

        def read(nodes, rows, lanes):
            x = sum(dot(part, lanes[...]) for part in thirds(nodes))
            return jnp.sum(x * rows[...], axis=0, keepdims=True)

        def spread(source, rows, lanes):
            x = rows[...]
            return sum(
                dot_rows((x * part.astype(F32)).astype(BF16), lanes[...]) for part in thirds(source)
            )

        def records(e):
            return read(e[0:4, 0:4, 0:4].reshape(64 * 8, ez), row_mask, lane_mask)

        def records_h(e):
            return read(e[4, 0:4, 0:4].reshape(16 * 8, ez), row_mask_h, lane_mask_h)

        fu, fl = force.at[0], force.at[1]
        for k in range(4):
            local[k].wait()
        order_own(0)
        local[4].wait()
        order_own(1)
        local[5].wait()
        set_stiffness()
        halo_wait([0])
        order_halo(0)
        fill(u.at[0])
        stencil(u.at[0], fu, store=grads.at[0])
        assemble(fu, 0)
        halo_wait([1])
        order_halo(1)
        fill(lam.at[0])
        stencil(lam.at[0], fl, store=grads.at[last])
        assemble(fl, steps)
        for k in range(6, 12):
            local[k].wait()
        for f in (2, 3, 4):
            order_own(f)
        halo_wait([2, 3, 4])
        for f in (2, 3, 4):
            order_halo(f)
        set_scale()
        share_all(0, sum(obs_ref[n] * obs_ref[n] for n in range(steps)))
        masks(rec_ref[...], row_mask, lane_mask, False)

        def sources_of(e, n):
            residual = records(e) - obs_ref[n - 1]
            residual_h = records_h(e) - halo_obs[n - 1]
            whole = spread(residual / mean_square, row_mask, lane_mask)
            inject[n - 1, 0:4] = whole.reshape(4, 4, 4, 8, ez)
            whole = spread(residual_h / mean_square, row_mask_h, lane_mask_h)
            inject[n - 1, 4] = whole.reshape(4, 4, 8, ez)
            return residual * residual

        residual_sum = jnp.zeros((1, ez), F32)
        receive(fu, 0)
        advance(u.at[1], u.at[0], before.at[0], fu)
        fill(u.at[1])
        for n in range(1, last):
            stencil(u.at[n], fu, store=grads.at[n])
            assemble(fu, n)
            if n == 1:
                halo_wait([5, 6])
                masks(halo_rec[...], row_mask_h, lane_mask_h, True)
                energy = take_all(0)
                mean_square = energy / samples + EPSILON
                receive(fl, steps)
            residual_sum = residual_sum + sources_of(u.at[n], n)
            receive(fu, n)
            advance(u.at[n + 1], u.at[n], u.at[n - 1], fu)
        residual_sum = residual_sum + sources_of(u.at[last], last)
        for k, n in enumerate(range(last, 0, -1)):
            for p in range(5):
                fl[p, 0:4, 0:4] = fl[p, 0:4, 0:4] - inject[n - 1, p]
            advance(lam.at[k + 1], lam.at[k], before.at[1] if k == 0 else lam.at[k - 1], fl)
            fill(lam.at[k + 1])
            if n - 1 > 0:
                stencil(lam.at[k + 1], fl, partner=grads.at[n - 1], fresh=k == 0)
                assemble(fl, steps + 1 + k)
                if k == 0:
                    fill(u.at[last])
                    stencil(u.at[last], fu, partner=grads.at[last])
                    assemble(fu, last)
                receive(fl, steps + 1 + k)
        stencil(lam.at[last], None, partner=grads.at[0])

        flat_total = total.reshape(125 * 8, ez)
        beside = event + 1 - 2 * lax.rem(event, 2)
        across = lax.rem(event + 2, events)
        beyond = lax.rem(beside + 2, events)
        for owner in range(events):
            for i in range(ex):
                pack[owner, i, 120:128] = jnp.zeros((8, ez), F32)
                pack[owner, i, 0:125] = flat_total[pl.ds(i * ey + owner, 125, stride=8), :]

        def reduce_copy(src, slot, there):
            return pltpu.make_async_remote_copy(
                src_ref=src, dst_ref=got.at[slot], send_sem=red_s.at[slot], recv_sem=red_r.at[slot],
                device_id={"event": there}, device_id_type=MESH,
            )

        first = reduce_copy(pack.at[beyond], 0, beside)
        second = reduce_copy(pack.at[beside], 1, beside)
        first.start()
        second.start()
        first.wait()
        relay[...] = pack[across] + got[0]
        third = reduce_copy(relay, 2, across)
        third.start()

        receive(fu, last)
        u3 = u.at[steps]
        advance(u3, u.at[last], u.at[last - 1] if last > 0 else before.at[0], fu, count=4)
        residual = records(u3) - obs_ref[last]
        share_all(1, residual_sum + residual * residual)

        @pl.when(has_left)
        def _():
            for copy in halo_copies:
                copy.wait_send()


        second.wait()
        pair_sum = pack[event] + got[1]
        third.wait()
        cube = jnp.broadcast_to(cube_ref[...][None], (ex, 128, ez))
        value = (pair_sum + got[2]) * cube
        final[...] = value

        top = jnp.max(jnp.abs(value).reshape(ex * 16, 8, ez), axis=0)
        tops_out[0] = top
        tops_in[event] = top
        for k in range(1, events):
            pltpu.make_async_remote_copy(
                src_ref=tops_out.at[0], dst_ref=tops_in.at[event],
                send_sem=top_s.at[k], recv_sem=top_r.at[event],
                device_id={"event": lax.rem(event + k, events)}, device_id_type=MESH,
            ).start()
        for k in range(1, events):
            there = lax.rem(event + k, events)
            copy = pltpu.make_async_remote_copy(
                src_ref=tops_out.at[0], dst_ref=tops_in.at[there],
                send_sem=top_s.at[k], recv_sem=top_r.at[there],
                device_id={"event": there}, device_id_type=MESH,
            )
            copy.wait_send()
            copy.wait_recv()
        top = jnp.max(tops_in[...], axis=0)
        tops_out[1] = top
        tops_far[me] = top

        @pl.loop(1, spaces)
        def _(k):
            pltpu.make_async_remote_copy(
                src_ref=tops_out.at[1], dst_ref=tops_far.at[me],
                send_sem=far_s.at[k], recv_sem=far_r.at[me],
                device_id={"space": lax.rem(me + k, spaces)}, device_id_type=MESH,
            ).start()

        misfit_sum = take_all(1)
        misfit_ref[...] = jnp.broadcast_to(
            0.5 * misfit_sum / (samples * mean_square), misfit_ref.shape
        )

        @pl.loop(1, spaces)
        def _(k):
            there = lax.rem(me + k, spaces)
            copy = pltpu.make_async_remote_copy(
                src_ref=tops_out.at[1], dst_ref=tops_far.at[there],
                send_sem=far_s.at[k], recv_sem=far_r.at[there],
                device_id={"space": there}, device_id_type=MESH,
            )
            copy.wait_send()
            copy.wait_recv()

        top = jnp.max(tops_far[...], axis=0)
        top = jnp.max(jnp.max(top, axis=1, keepdims=True), axis=0, keepdims=True)
        inverse = 1.0 / (top + EPSILON)
        final[...] = final[...] * inverse[None]
        for p in range(5):
            for i in range(ex):
                for q in range(5):
                    at = (p * 5 + q) * 5
                    out_ref[p, i, q, 0] = final[i, at : at + 5, :]

    return kernel


def shards(mesh_shape, now, prev, adj, nxt, modulus, density, receivers, observed):
    events, spaces = mesh_shape["event"], mesh_shape["space"]
    ex, ey, ez = modulus.shape[1], modulus.shape[3], modulus.shape[5]
    steps, count = observed.shape[1], receivers.shape[0]
    assert ex * ey == 8 and ex == 2 and ez == 128 and count == 128 and events == 4 == ey
    assert steps >= 3 and now.shape[0] == 1
    ny, nz = now.shape[2], now.shape[3]
    column, rows, plane, cube = tables(ex, ey, ez)
    kernel = make_kernel(ex, ey, ez, steps, events, spaces, count * spaces)
    vm = lambda *shape: pltpu.VMEM(shape, F32)
    dma = lambda *shape: pltpu.SemaphoreType.DMA(shape)
    rounds = 2 * steps
    scratch = [
        vm(5, 4 * ex, ny, nz), vm(5, ex, 5, 5, ey, ez), pltpu.VMEM((1, count), jnp.int32),
        vm(steps, 1, count), pltpu.VMEM(column.shape, BF16), pltpu.VMEM(rows.shape, BF16),
        pltpu.VMEM(plane.shape, BF16), vm(*cube.shape), dma(12),
        vm(5, ny, nz), pltpu.VMEM((1, count), jnp.int32), vm(steps, 1, count),
        vm(steps + 1, 5, 5, 5, 8, ez), vm(steps, 5, 5, 5, 8, ez), vm(2, 5, 4, 4, 8, ez),
        vm(5, 4, 4, 8, ez), vm(5, 5, 5, 8, ez), vm(steps, 3, 5, 5, 5, 8, ez),
        vm(2, 5, 5, 5, 8, ez), vm(5, 5, 5, 8, ez), vm(steps - 1, 5, 4, 4, 8, ez),
        vm(512, count), pltpu.VMEM((ez, count), BF16), vm(128, count),
        pltpu.VMEM((ez, count), BF16),
        vm(rounds, 2, 4, 8, ez), vm(rounds, 2, 4, 8, ez),
        vm(rounds, 2, 4, 8, ez), vm(rounds, 2, 4, 8, ez),
        vm(2, 8, ez), vm(2, spaces, 8, ez), vm(events, ex, 128, ez), vm(3, ex, 128, ez),
        vm(ex, 128, ez), vm(2, 8, ez), vm(events, 8, ez), vm(spaces, 8, ez), vm(ex, 128, ez),
        dma(7), dma(7), dma(rounds), dma(rounds), dma(rounds), dma(rounds),
        dma(2, spaces), dma(2, spaces), dma(3), dma(3),
        dma(events), dma(events), dma(spaces), dma(spaces),
    ]
    vmem = pl.BlockSpec(memory_space=pltpu.VMEM)
    hbm = pl.BlockSpec(memory_space=pltpu.HBM)
    out, misfit = pl.pallas_call(
        kernel,
        out_shape=(
            jax.ShapeDtypeStruct((5, ex, 5, ey // events, 5, ez), F32),
            jax.ShapeDtypeStruct((1, ez), F32),
        ),
        in_specs=[hbm] * 12,
        out_specs=(vmem, vmem),
        scratch_shapes=scratch,
        compiler_params=pltpu.CompilerParams(
            collective_id=0, has_side_effects=True, vmem_limit_bytes=LIMIT
        ),
        name="window",
    )(
        now, prev, adj, nxt, density, jnp.transpose(modulus, (0, 1, 2, 4, 3, 5)),
        receivers.reshape(1, count), jnp.transpose(observed, (1, 0, 2)),
        jnp.asarray(column), jnp.asarray(rows), jnp.asarray(plane), jnp.asarray(cube),
    )
    return out, misfit[0, :1]


def solution(mesh):
    in_specs = (
        P("event", "space", None, None),
        P("event", "space", None, None),
        P("event", "space", None, None),
        P("event", "space", None, None),
        P(None, "space", None, None, None, None),
        P("space", None, None),
        P("space"),
        P("event", None, "space"),
    )
    out_specs = (P(None, "space", None, "event", None, None), P("event"))
    sizes = dict(mesh.shape)

    def program(*args):
        return shards(sizes, *args)

    return jax.shard_map(program, mesh=mesh, in_specs=in_specs, out_specs=out_specs, check_vma=False)
```

profile of v0, /device:TPU:0, one launch (start us, length us, event | category | flops | bytes accessed | tf_op | source)
XLA Modules:
  0.0 42.2 jit_solution(8121058611198003117)
XLA Ops:
  0.6 38.6 %window.1 = (f32[5,2,5,1,5,128]{5,4,3,2,1,0:T(8,128)}, f32[1,128]{1,0:T(1,128)}) custom-call(f32[1,8,16,512]{3,2,1,0:T(8,128)} %now_hbm.1, f32[1,8,16,512]{3,2,1,0:T(8,128)} %prev_hbm.1, f32[1,8,16,512]{3,2,1,0:T(8,128)} %adj_hbm.1, f32[1,8,16,512]{3,2,1,0:T(8,128)} %next_hbm.1, f32[8,16,512]{2,1,0:T(8,128)} %density_hbm.1, ...), custom_call_target="tpu_custom_call" | custom-call | tf_op jit(solution)/shard_map/window/pallas_call | solution.py:636
  39.3 0.0 copy-start
  39.3 1.7 %copy.14 = f32[5,2,5,1,5,128]{5,3,4,2,1,0:T(1,128)} copy(f32[5,2,5,1,5,128]{5,4,3,2,1,0:T(8,128)} %get-tuple-element.6) | data formatting | bytes 256000
  41.0 0.0 copy-done
Async XLA Ops:
  39.3 1.7 %copy-start = (f32[1,128]{1,0:T(1,128)S(1)}, f32[1,128]{1,0:T(1,128)}, u32[]{:S(2)}) copy-start(f32[1,128]{1,0:T(1,128)} %get-tuple-element.5) | copy-start | bytes 1540
where the time goes:
time: 42.3 us; the launch traced here: 42.2 us
  Pallas kernels  38.6 us (91%)
  between operations  1.81 us (4%)
  local copies, waits for them, and re-layouts  1.72 us (4%)
    pallas_call x1, Pallas kernels, shards(): pl.pallas_call(kernel, out_shape=(jax.ShapeDtypeStruct((5, ex, 5, ey // e...  38.6 us
    unnamed x3, local copies, waits for them, and re-layouts  1.72 us

commit v1 on v0

--- a/solution.py
+++ b/solution.py
@@ -2,7 +2,6 @@
 
 import jax
 import jax.numpy as jnp
-import ml_dtypes
 import numpy as np
 from jax import lax
 from jax.experimental import pallas as pl
@@ -69,27 +68,6 @@
     return lax.dot_general(a, b, (((1,), (1,)), ((), ())), preferred_element_type=F32)
 
 
-def tables(ex, ey, ez):
-    ny, nz = 4 * ey, 4 * ez
-    column = np.zeros((nz, nz), np.float32)
-    for r in range(4):
-        for l in range(ez):
-            column[4 * l + r, r * ez + l] = 1
-    rows = np.zeros((4 * ex * ny, 4 * ex * ny), np.float32)
-    plane = np.zeros((32, ny), np.float32)
-    for q in range(4):
-        for j in range(ey):
-            for i in range(ex):
-                for p in range(4):
-                    rows[(p * 4 + q) * 8 + i * ey + j, (i * 4 + p) * ny + j * 4 + q] = 1
-            plane[q * 8 + (ex - 1) * ey + j, j * 4 + q] = 1
-    cube = np.zeros((128, ez), np.float32)
-    w = WEIGHTS
-    cube[:125] = -(w[:, None, None] * w[None, :, None] * w[None, None, :]).reshape(125, 1)
-    as_bf16 = [t.astype(ml_dtypes.bfloat16) for t in (column, rows, plane)]
-    return as_bf16 + [cube]
-
-
 def make_kernel(ex, ey, ez, steps, events, spaces, receivers_total):
     ny, nz = 4 * ey, 4 * ez
     half = (ex - 1) * ey
@@ -101,9 +79,8 @@
 
     def kernel(
         now_hbm, prev_hbm, adj_hbm, next_hbm, density_hbm, modulus_hbm, rec_hbm, obs_hbm,
-        column_hbm, rows_hbm, plane_hbm, cube_hbm,
         out_ref, misfit_ref,
-        fields, modulus_ref, rec_ref, obs_ref, column_ref, rows_ref, plane_ref, cube_ref, in_sem,
+        fields, modulus_ref, rec_ref, obs_ref, column_ref, sorted_rows, cube_ref, in_sem,
         halo, halo_rec, halo_obs, u, lam, before, scale, stiff, grads, force, total, inject,
         row_mask, lane_mask, row_mask_h, lane_mask_h,
         send_l, send_r, recv_l, recv_r, sums_out, sums_in, pack, got, relay, tops_out, tops_in, tops_far,
@@ -117,11 +94,12 @@
         has_left, has_right = me > 0, me < spaces - 1
         MESH = pl.DeviceIdType.MESH
 
+        def iota(shape, axis):
+            return lax.broadcasted_iota(jnp.int32, shape, axis)
+
         own = [r.at[0] for r in (now_hbm, adj_hbm, prev_hbm, next_hbm)] + [density_hbm]
-        local = [(own[0], fields.at[0]), (rows_hbm, rows_ref), (column_hbm, column_ref)]
-        local += [(plane_hbm, plane_ref), (own[1], fields.at[1]), (modulus_hbm, modulus_ref)]
-        local += [(own[f], fields.at[f]) for f in (2, 3, 4)]
-        local += [(rec_hbm, rec_ref), (obs_hbm, obs_ref), (cube_hbm, cube_ref)]
+        local = [(own[f], fields.at[f]) for f in range(5)]
+        local += [(modulus_hbm, modulus_ref), (rec_hbm, rec_ref), (obs_hbm, obs_ref)]
         local = [
             pltpu.make_async_copy(src, dst, in_sem.at[k]) for k, (src, dst) in enumerate(local)
         ]
@@ -139,8 +117,23 @@
                 barrier, inc=1, device_id={"event": lax.rem(event + k, events)}, device_id_type=MESH
             )
 
-        for copy in local:
-            copy.start()
+        for k in (0, 5, 2, 4, 1, 3, 6, 7):
+            local[k].start()
+
+        width = 2 * ez
+        z, c = iota((width, width), 0), iota((width, width), 1)
+        hit = z == 4 * (c & (width // 4 - 1)) + lax.shift_right_logical(c, shift_y - 3)
+        column_ref[...] = jnp.where(hit, 1.0, 0.0).astype(BF16)
+
+        def at_point(x):
+            edge = jnp.logical_or(x == 0, x == 4)
+            w = jnp.where(edge, WEIGHTS[0], jnp.where(x == 2, WEIGHTS[2], WEIGHTS[1]))
+            return w.astype(F32)
+
+        point = iota((128, ez), 0)
+        p = lax.shift_right_logical(point * 41, 10)
+        q = lax.shift_right_logical((point - 25 * p) * 205, 10)
+        cube_ref[...] = -at_point(p) * at_point(q) * at_point(point - 25 * p - 5 * q)
 
         @pl.when(jnp.logical_not(has_right))
         def _():
@@ -176,8 +169,7 @@
 
         @pl.when(has_left)
         def _():
-            for copy in halo_copies:
-                copy.start()
+            halo_copies[0].start()
 
         def halo_wait(numbers):
             @pl.when(has_right)
@@ -220,31 +212,44 @@
             tile = jnp.sum(sums_in[slot], axis=0)
             return jnp.sum(tile[0:1, :], axis=1, keepdims=True)
 
-        def iota(shape, axis):
-            return lax.broadcasted_iota(jnp.int32, shape, axis)
-
         def target(f):
             if f < 2:
                 return (u, lam)[f].at[0]
             return before.at[f - 2] if f < 4 else scale
 
-        def order(nodes, rows):
-            count = rows.shape[0]
-            parts = [dot(rows[...], part).astype(BF16) for part in thirds(nodes)]
-            x = dot(jnp.concatenate(parts, axis=0), column_ref[...])
-            return x[:count] + x[count : 2 * count] + x[2 * count :]
+        def sort_columns(nodes):
+            count = nodes.shape[0]
+            parts = thirds(nodes)
+            halves = [part[:, h * width : (h + 1) * width] for h in range(2) for part in parts]
+            x = dot(jnp.concatenate(halves, axis=0), column_ref[...])
+            x = [x[k * count : (k + 1) * count] for k in range(6)]
+            near, far = x[0] + x[1] + x[2], x[3] + x[4] + x[5]
+            lower = iota((count, ez), 1) < ez // 2
+            for pair in range(2):
+                a = near[:, pair * ez : (pair + 1) * ez]
+                b = far[:, pair * ez : (pair + 1) * ez]
+                sorted_rows[2 * pair, 0:count] = jnp.where(lower, a, pltpu.roll(b, ez // 2, 1))
+                sorted_rows[2 * pair + 1, 0:count] = jnp.where(lower, pltpu.roll(a, ez // 2, 1), b)
 
         def order_own(f):
-            values = order(fields[f].reshape(4 * ex * ny, nz), rows_ref)
+            local[f].wait()
+            sort_columns(fields[f].reshape(4 * ex * ny, nz))
             for r in range(4):
-                part = values[:, r * ez : (r + 1) * ez]
-                target(f)[0:4, 0:4, r] = part.reshape(4, 4, 8, ez)
+                rows = sorted_rows.at[r]
+                for p in range(4):
+                    for q in range(4):
+                        for i in range(ex):
+                            picked = rows[pl.ds((i * 4 + p) * ny + q, ey, stride=4), :]
+                            target(f)[p, q, r, i * ey : (i + 1) * ey, :] = picked
 
         def order_halo(f):
-            values = order(halo[f], plane_ref)
+            halo_wait([f])
+            sort_columns(halo[f])
+            target(f)[4, 0:4, 0:4] = jnp.zeros((4, 4, 8, ez), F32)
             for r in range(4):
-                part = values[:, r * ez : (r + 1) * ez]
-                target(f)[4, 0:4, r] = part.reshape(4, 8, ez)
+                rows = sorted_rows.at[r]
+                for q in range(4):
+                    target(f)[4, q, r, half : half + ey, :] = rows[pl.ds(q, ey, stride=4), :]
 
         def set_stiffness():
             for p in range(5):
@@ -430,33 +435,29 @@
             return read(e[4, 0:4, 0:4].reshape(16 * 8, ez), row_mask_h, lane_mask_h)
 
         fu, fl = force.at[0], force.at[1]
-        for k in range(4):
-            local[k].wait()
         order_own(0)
-        local[4].wait()
-        order_own(1)
+
+        @pl.when(has_left)
+        def _():
+            for k in (2, 4, 1, 3, 5, 6):
+                halo_copies[k].start()
+
         local[5].wait()
         set_stiffness()
-        halo_wait([0])
         order_halo(0)
         fill(u.at[0])
         stencil(u.at[0], fu, store=grads.at[0])
         assemble(fu, 0)
-        halo_wait([1])
+        for f in (2, 4):
+            order_own(f)
+            order_halo(f)
+        set_scale()
+        order_own(1)
         order_halo(1)
         fill(lam.at[0])
-        stencil(lam.at[0], fl, store=grads.at[last])
-        assemble(fl, steps)
-        for k in range(6, 12):
-            local[k].wait()
-        for f in (2, 3, 4):
-            order_own(f)
-        halo_wait([2, 3, 4])
-        for f in (2, 3, 4):
-            order_halo(f)
-        set_scale()
+        local[6].wait()
+        local[7].wait()
         share_all(0, sum(obs_ref[n] * obs_ref[n] for n in range(steps)))
-        masks(rec_ref[...], row_mask, lane_mask, False)
 
         def sources_of(e, n):
             residual = records(e) - obs_ref[n - 1]
@@ -475,15 +476,21 @@
             stencil(u.at[n], fu, store=grads.at[n])
             assemble(fu, n)
             if n == 1:
+                stencil(lam.at[0], fl, store=grads.at[last])
+                assemble(fl, steps)
+                order_own(3)
+                order_halo(3)
+                masks(rec_ref[...], row_mask, lane_mask, False)
                 halo_wait([5, 6])
                 masks(halo_rec[...], row_mask_h, lane_mask_h, True)
                 energy = take_all(0)
                 mean_square = energy / samples + EPSILON
-                receive(fl, steps)
             residual_sum = residual_sum + sources_of(u.at[n], n)
             receive(fu, n)
             advance(u.at[n + 1], u.at[n], u.at[n - 1], fu)
         residual_sum = residual_sum + sources_of(u.at[last], last)
+        receive(fl, steps)
+
         for k, n in enumerate(range(last, 0, -1)):
             for p in range(5):
                 fl[p, 0:4, 0:4] = fl[p, 0:4, 0:4] - inject[n - 1, p]
@@ -538,8 +545,7 @@
         second.wait()
         pair_sum = pack[event] + got[1]
         third.wait()
-        cube = jnp.broadcast_to(cube_ref[...][None], (ex, 128, ez))
-        value = (pair_sum + got[2]) * cube
+        value = (pair_sum + got[2]) * cube_ref[...][None]
         final[...] = value
 
         top = jnp.max(jnp.abs(value).reshape(ex * 16, 8, ez), axis=0)
@@ -594,9 +600,8 @@
         final[...] = final[...] * inverse[None]
         for p in range(5):
             for i in range(ex):
-                for q in range(5):
-                    at = (p * 5 + q) * 5
-                    out_ref[p, i, q, 0] = final[i, at : at + 5, :]
+                at = (p * ex + i) * 25
+                out_ref[at : at + 25, :] = final[i, p * 25 : p * 25 + 25, :]
 
     return kernel
 
@@ -608,15 +613,14 @@
     assert ex * ey == 8 and ex == 2 and ez == 128 and count == 128 and events == 4 == ey
     assert steps >= 3 and now.shape[0] == 1
     ny, nz = now.shape[2], now.shape[3]
-    column, rows, plane, cube = tables(ex, ey, ez)
     kernel = make_kernel(ex, ey, ez, steps, events, spaces, count * spaces)
     vm = lambda *shape: pltpu.VMEM(shape, F32)
     dma = lambda *shape: pltpu.SemaphoreType.DMA(shape)
     rounds = 2 * steps
     scratch = [
         vm(5, 4 * ex, ny, nz), vm(5, ex, 5, 5, ey, ez), pltpu.VMEM((1, count), jnp.int32),
-        vm(steps, 1, count), pltpu.VMEM(column.shape, BF16), pltpu.VMEM(rows.shape, BF16),
-        pltpu.VMEM(plane.shape, BF16), vm(*cube.shape), dma(12),
+        vm(steps, 1, count), pltpu.VMEM((2 * ez, 2 * ez), BF16), vm(4, 4 * ex * ny, ez),
+        vm(128, ez), dma(8),
         vm(5, ny, nz), pltpu.VMEM((1, count), jnp.int32), vm(steps, 1, count),
         vm(steps + 1, 5, 5, 5, 8, ez), vm(steps, 5, 5, 5, 8, ez), vm(2, 5, 4, 4, 8, ez),
         vm(5, 4, 4, 8, ez), vm(5, 5, 5, 8, ez), vm(steps, 3, 5, 5, 5, 8, ez),
@@ -636,10 +640,10 @@
     out, misfit = pl.pallas_call(
         kernel,
         out_shape=(
-            jax.ShapeDtypeStruct((5, ex, 5, ey // events, 5, ez), F32),
+            jax.ShapeDtypeStruct((25 * 5 * ex, ez), F32),
             jax.ShapeDtypeStruct((1, ez), F32),
         ),
-        in_specs=[hbm] * 12,
+        in_specs=[hbm] * 8,
         out_specs=(vmem, vmem),
         scratch_shapes=scratch,
         compiler_params=pltpu.CompilerParams(
@@ -649,9 +653,9 @@
     )(
         now, prev, adj, nxt, density, jnp.transpose(modulus, (0, 1, 2, 4, 3, 5)),
         receivers.reshape(1, count), jnp.transpose(observed, (1, 0, 2)),
-        jnp.asarray(column), jnp.asarray(rows), jnp.asarray(plane), jnp.asarray(cube),
     )
-    return out, misfit[0, :1]
+    out = out.reshape(5, ex, 5, 5, 1, ez)
+    return jnp.transpose(out, (0, 1, 2, 4, 3, 5)), misfit[0, :1]
 
 
 def solution(mesh):

time: 42.3 us -> 41.6 us (0.983)
  Pallas kernels: 38.6 us -> 37.9 us
    unnamed x3 -> x2, local copies, waits for them, and re-layouts: 1.72 us -> 0.01 us
    another operation x0 -> x1, local copies, waits for them, and re-layouts: none -> 1.68 us  [shards(): return (jnp.transpose(out, (0, 1, 2, 4, 3, 5)), misfit[0, :1])]
    pallas_call x1, Pallas kernels: 38.6 us -> 37.9 us  [shards(): pl.pallas_call(kernel, out_shape=(jax.ShapeDtypeStruct((25 * 5 * ex, ez),...]
where the time goes in v1:
time: 41.6 us; the launch traced here: 41.4 us
  Pallas kernels  37.9 us (91%)
  between operations  1.81 us (4%)
  local copies, waits for them, and re-layouts  1.68 us (4%)
    pallas_call x1, Pallas kernels, shards(): pl.pallas_call(kernel, out_shape=(jax.ShapeDtypeStruct((25 * 5 * ex, ez),...  37.9 us
    another operation x1, local copies, waits for them, and re-layouts, shards(): return (jnp.transpose(out, (0, 1, 2, 4, 3, 5)), misfit[0, :1])  1.68 us

profile of v1, /device:TPU:0, one launch (start us, length us, event | category | flops | bytes accessed | tf_op | source)
XLA Modules:
  0.0 41.4 jit_solution(9744131532306529543)
XLA Ops:
  0.6 37.9 %window.1 = (f32[250,128]{1,0:T(8,128)}, f32[1,128]{1,0:T(1,128)}) custom-call(f32[1,8,16,512]{3,2,1,0:T(8,128)} %now_hbm.1, f32[1,8,16,512]{3,2,1,0:T(8,128)} %prev_hbm.1, f32[1,8,16,512]{3,2,1,0:T(8,128)} %adj_hbm.1, f32[1,8,16,512]{3,2,1,0:T(8,128)} %next_hbm.1, f32[8,16,512]{2,1,0:T(8,128)} %density_hbm.1, f32[5,2,5,5,4,128]{5,4,3,2,1,0:T(4,128)} %bitcast.5, ...), custom_call_target="tpu_custom_call" | custom-call | tf_op jit(solution)/shard_map/window/pallas_call | solution.py:640
  38.6 0.0 copy-start
  38.6 1.7 %transpose_reshape.4 = f32[5,2,5,1,5,128]{5,3,4,2,1,0:T(1,128)} reshape(f32[250,128]{1,0:T(8,128)} %get-tuple-element.4) | data formatting | bytes 256000 | tf_op jit(solution)/shard_map/transpose;reshape | solution.py:658
  40.3 0.0 copy-done
Async XLA Ops:
  38.6 1.7 %copy-start = (f32[1,128]{1,0:T(1,128)S(1)}, f32[1,128]{1,0:T(1,128)}, u32[]{:S(2)}) copy-start(f32[1,128]{1,0:T(1,128)} %get-tuple-element.5) | copy-start | bytes 1540

commit v2 on v1

--- a/solution.py
+++ b/solution.py
@@ -79,13 +79,13 @@
 
     def kernel(
         now_hbm, prev_hbm, adj_hbm, next_hbm, density_hbm, modulus_hbm, rec_hbm, obs_hbm,
-        out_ref, misfit_ref,
+        out_hbm, side_ref,
         fields, modulus_ref, rec_ref, obs_ref, column_ref, sorted_rows, cube_ref, in_sem,
         halo, halo_rec, halo_obs, u, lam, before, scale, stiff, grads, force, total, inject,
         row_mask, lane_mask, row_mask_h, lane_mask_h,
         send_l, send_r, recv_l, recv_r, sums_out, sums_in, pack, got, relay, tops_out, tops_in, tops_far,
         final,
-        halo_ss, halo_rs, ls, lr, rs, rr, sum_s, sum_r, red_s, red_r, top_s, top_r, far_s, far_r,
+        out_sem, halo_ss, halo_rs, ls, lr, rs, rr, sum_s, sum_r, red_s, red_r, top_s, top_r, far_s, far_r,
     ):
         me = lax.axis_index("space")
         event = lax.axis_index("event")
@@ -439,8 +439,8 @@
 
         @pl.when(has_left)
         def _():
-            for k in (2, 4, 1, 3, 5, 6):
-                halo_copies[k].start()
+            halo_copies[4].start()
+            halo_copies[2].start()
 
         local[5].wait()
         set_stiffness()
@@ -448,13 +448,17 @@
         fill(u.at[0])
         stencil(u.at[0], fu, store=grads.at[0])
         assemble(fu, 0)
-        for f in (2, 4):
+
+        @pl.when(has_left)
+        def _():
+            for k in (1, 5, 6, 3):
+                halo_copies[k].start()
+
+        for f in (4, 2):
             order_own(f)
             order_halo(f)
         set_scale()
         order_own(1)
-        order_halo(1)
-        fill(lam.at[0])
         local[6].wait()
         local[7].wait()
         share_all(0, sum(obs_ref[n] * obs_ref[n] for n in range(steps)))
@@ -476,6 +480,8 @@
             stencil(u.at[n], fu, store=grads.at[n])
             assemble(fu, n)
             if n == 1:
+                order_halo(1)
+                fill(lam.at[0])
                 stencil(lam.at[0], fl, store=grads.at[last])
                 assemble(fl, steps)
                 order_own(3)
@@ -546,7 +552,12 @@
         pair_sum = pack[event] + got[1]
         third.wait()
         value = (pair_sum + got[2]) * cube_ref[...][None]
-        final[...] = value
+        for p in range(5):
+            for i in range(ex):
+                at = (p * ex + i) * 25
+                final[at : at + 25, 0, :] = value[i, p * 25 : p * 25 + 25, :]
+        out_copy = pltpu.make_async_copy(final, out_hbm, out_sem)
+        out_copy.start()
 
         top = jnp.max(jnp.abs(value).reshape(ex * 16, 8, ez), axis=0)
         tops_out[0] = top
@@ -579,9 +590,8 @@
             ).start()
 
         misfit_sum = take_all(1)
-        misfit_ref[...] = jnp.broadcast_to(
-            0.5 * misfit_sum / (samples * mean_square), misfit_ref.shape
-        )
+        misfit = 0.5 * misfit_sum / (samples * mean_square)
+        side_ref[0:1] = jnp.broadcast_to(misfit, (1, ez))
 
         @pl.loop(1, spaces)
         def _(k):
@@ -596,12 +606,8 @@
 
         top = jnp.max(tops_far[...], axis=0)
         top = jnp.max(jnp.max(top, axis=1, keepdims=True), axis=0, keepdims=True)
-        inverse = 1.0 / (top + EPSILON)
-        final[...] = final[...] * inverse[None]
-        for p in range(5):
-            for i in range(ex):
-                at = (p * ex + i) * 25
-                out_ref[at : at + 25, :] = final[i, p * 25 : p * 25 + 25, :]
+        side_ref[1:2] = jnp.broadcast_to(1.0 / (top + EPSILON), (1, ez))
+        out_copy.wait()
 
     return kernel
 
@@ -630,21 +636,22 @@
         vm(rounds, 2, 4, 8, ez), vm(rounds, 2, 4, 8, ez),
         vm(rounds, 2, 4, 8, ez), vm(rounds, 2, 4, 8, ez),
         vm(2, 8, ez), vm(2, spaces, 8, ez), vm(events, ex, 128, ez), vm(3, ex, 128, ez),
-        vm(ex, 128, ez), vm(2, 8, ez), vm(events, 8, ez), vm(spaces, 8, ez), vm(ex, 128, ez),
+        vm(ex, 128, ez), vm(2, 8, ez), vm(events, 8, ez), vm(spaces, 8, ez), vm(25 * 5 * ex, 1, ez),
+        pltpu.SemaphoreType.DMA,
         dma(7), dma(7), dma(rounds), dma(rounds), dma(rounds), dma(rounds),
         dma(2, spaces), dma(2, spaces), dma(3), dma(3),
         dma(events), dma(events), dma(spaces), dma(spaces),
     ]
     vmem = pl.BlockSpec(memory_space=pltpu.VMEM)
     hbm = pl.BlockSpec(memory_space=pltpu.HBM)
-    out, misfit = pl.pallas_call(
+    out, side = pl.pallas_call(
         kernel,
         out_shape=(
-            jax.ShapeDtypeStruct((25 * 5 * ex, ez), F32),
-            jax.ShapeDtypeStruct((1, ez), F32),
+            jax.ShapeDtypeStruct((25 * 5 * ex, 1, ez), F32),
+            jax.ShapeDtypeStruct((2, ez), F32),
         ),
         in_specs=[hbm] * 8,
-        out_specs=(vmem, vmem),
+        out_specs=(hbm, vmem),
         scratch_shapes=scratch,
         compiler_params=pltpu.CompilerParams(
             collective_id=0, has_side_effects=True, vmem_limit_bytes=LIMIT
@@ -654,8 +661,8 @@
         now, prev, adj, nxt, density, jnp.transpose(modulus, (0, 1, 2, 4, 3, 5)),
         receivers.reshape(1, count), jnp.transpose(observed, (1, 0, 2)),
     )
-    out = out.reshape(5, ex, 5, 5, 1, ez)
-    return jnp.transpose(out, (0, 1, 2, 4, 3, 5)), misfit[0, :1]
+    out = jnp.transpose(out.reshape(5, ex, 5, 5, 1, ez), (0, 1, 2, 4, 3, 5))
+    return out * side[1, 0], side[0, :1]
 
 
 def solution(mesh):

time: 41.6 us -> 42.3 us (1.017)
  other arithmetic: 0 us -> 2.27 us
  between operations: 1.81 us -> 0.65 us
  local copies, waits for them, and re-layouts: 1.68 us -> 1.17 us
    mul x0 -> x1, other arithmetic: none -> 2.27 us  [shards(): return (out * side[1, 0], side[0, :1])]
    another operation x1 -> x0, local copies, waits for them, and re-layouts: 1.68 us -> none  [shards(): return (jnp.transpose(out, (0, 1, 2, 4, 3, 5)), misfit[0, :1])]
    unnamed x2, local copies, waits for them, and re-layouts: 0.01 us -> 0.63 us
    slice x0 -> x1, local copies, waits for them, and re-layouts: none -> 0.54 us  [shards(): return (out * side[1, 0], side[0, :1])]
where the time goes in v2:
time: 42.3 us; the launch traced here: 42.1 us
  Pallas kernels  38 us (90%)
  other arithmetic  2.27 us (5%)
  local copies, waits for them, and re-layouts  1.17 us (3%)
  between operations  0.65 us (2%)
    pallas_call x1, Pallas kernels, shards(): pl.pallas_call(kernel, out_shape=(jax.ShapeDtypeStruct((25 * 5 * ex, 1, e...  38 us
    mul x1, other arithmetic, shards(): return (out * side[1, 0], side[0, :1])  2.27 us

profile of v2, /device:TPU:0, one launch (start us, length us, event | category | flops | bytes accessed | tf_op | source)
XLA Modules:
  0.0 42.1 jit_solution(14252554032561073945)
XLA Ops:
  0.6 38.0 %window.1 = (f32[250,1,128]{2,1,0:T(1,128)}, f32[2,128]{1,0:T(2,128)}) custom-call(f32[1,8,16,512]{3,2,1,0:T(8,128)} %now_hbm.1, f32[1,8,16,512]{3,2,1,0:T(8,128)} %prev_hbm.1, f32[1,8,16,512]{3,2,1,0:T(8,128)} %adj_hbm.1, f32[1,8,16,512]{3,2,1,0:T(8,128)} %next_hbm.1, f32[8,16,512]{2,1,0:T(8,128)} %density_hbm.1, f32[5,2,5,5,4,128]{5,4,3,2,1,0:T(4,128)} %bitcast.6, ...), custom_call_target="tpu_custom_call" | custom-call | tf_op jit(solution)/shard_map/window/pallas_call | solution.py:647
  38.7 0.0 copy-start
  38.7 0.6 %copy-done = f32[2,128]{1,0:T(2,128)S(1)} copy-done((f32[2,128]{1,0:T(2,128)S(1)}, f32[2,128]{1,0:T(2,128)}, u32[]{:S(2)}) %copy-start) | copy-done | bytes 1048
  39.3 0.5 %fusion = (f32[1,1]{1,0:T(1,128)}, f32[1,1]{1,0:T(1,128)}) fusion(f32[2,128]{1,0:T(2,128)S(1)} %copy-done), kind=kLoop, calls=%fused_computation.1 | loop fusion | bytes 16 | tf_op jit(solution)/shard_map/slice | solution.py:665
  39.8 2.3 %broadcast_multiply_fusion = f32[250,1,128]{2,1,0:T(1,128)} fusion(f32[250,1,128]{2,1,0:T(1,128)} %get-tuple-element.4, f32[]{:T(128)} %bitcast.3), kind=kLoop, calls=%fused_computation | loop fusion | flops 32000 | bytes 256004 | tf_op jit(solution)/shard_map/mul | solution.py:665
Async XLA Ops:
  38.7 0.6 %copy-start = (f32[2,128]{1,0:T(2,128)S(1)}, f32[2,128]{1,0:T(2,128)}, u32[]{:S(2)}) copy-start(f32[2,128]{1,0:T(2,128)} %get-tuple-element.5) | copy-start | bytes 3076
